TPU v7x, 32 devices: a whole 2x2x4 slice. The times are simulated.
32 devices in a mesh: dp: 4 (over y, x), tensor: 8 (over z, core).
Axes of the slice: x: 2, y: 2, z: 4, core: 2. Of those that a mesh axis runs over, the one named last changes fastest.
Arguments:
- hidden: bfloat16 [3072, 20480], P('dp', 'tensor'), may hold values from -6 to 6
- out_grad: bfloat16 [3072, 8192], P('dp', 'tensor'), may hold values from -6 to 6
- w_down: bfloat16 [20480, 8192], P('tensor'), may hold values from -0.0625 to 0.0625
- proj_in: bfloat16 [64, 20480], P(None, 'tensor'), may hold values from -0.0390625 to 0.0390625
- proj_out: bfloat16 [64, 8192], P(None, 'tensor'), may hold values from -0.0625 to 0.0625
- queries: bfloat16 [1024, 4096], P('tensor'), may hold values from -0.005859375 to 0.005859375
- assignment: int32 [12], replicated, may hold values from 0 to 7
Outputs:
- input_grad: bfloat16 [3072, 20480], P('dp', 'tensor')
- scores: float32 [8, 1024], P('dp', 'tensor')
All inputs are finite; a program needn't handle non-finite values.
Results may differ from a plain program's by a relative error of at most 0.001.
Values may be sent and summed in bfloat16 or wider, within the bound.
A program may use at most 128 MiB of HBM per device.

v0:
```python
import jax
import jax.numpy as jnp
from jax import lax
from jax.sharding import PartitionSpec as P

LEN = 256
EX_DEV = 2


def on_device(hidden, out_grad, w_down, proj_in, proj_out, queries, assignment):
    tok_rows = hidden.shape[0]
    seq_count = tok_rows // LEN
    act_part = jnp.einsum("tf,kf->tk", hidden, proj_in, preferred_element_type=jnp.float32)
    grad_piece = lax.all_gather(out_grad, "tensor", axis=1, tiled=True)
    proj_piece = lax.all_gather(proj_out, "tensor", axis=1, tiled=True)
    first = jnp.einsum("td,fd->tf", grad_piece, w_down, preferred_element_type=jnp.float32)
    second = jnp.einsum("td,kd->tk", grad_piece, proj_piece, preferred_element_type=jnp.float32)
    act_low = lax.psum(act_part, "tensor")
    input_grad = first.astype(jnp.bfloat16)
    width = act_low.shape[1]
    act_seq = act_low.reshape(seq_count, LEN, width)
    grad_seq = second.reshape(seq_count, LEN, width)
    proj_grads = jnp.einsum(
        "slk,slm->skm", act_seq, grad_seq, precision=lax.Precision.HIGHEST
    ).reshape(seq_count, width * width)
    query_wide = queries.astype(jnp.float32)
    all_grads = lax.all_gather(proj_grads, "dp", axis=0, tiled=True)
    first_example = lax.axis_index("dp") * EX_DEV
    example_ids = first_example + jnp.arange(EX_DEV, dtype=jnp.int32)
    one_hot = (example_ids[:, None] == assignment[None, :]).astype(jnp.float32)
    example_grads = jnp.dot(one_hot, all_grads, precision=lax.Precision.HIGHEST)
    scores = jnp.dot(example_grads, query_wide.T, precision=lax.Precision.HIGHEST)
    return (input_grad, scores)


def solution(mesh):
    placed = (
        P("dp", "tensor"),
        P("dp", "tensor"),
        P("tensor", None),
        P(None, "tensor"),
        P(None, "tensor"),
        P("tensor", None),
        P(),
    )
    return jax.shard_map(
        on_device,
        mesh=mesh,
        in_specs=placed,
        out_specs=(P("dp", "tensor"), P("dp", "tensor")),
        check_vma=False,
    )
```

profile of v0, /device:TPU:0, one launch (start us, length us, event | category | flops | bytes accessed | tf_op | source)
XLA Modules:
  0.0 268.6 jit_solution(14514635404647256841)
XLA Ops:
  7.2 0.0 copy-start
  7.2 0.0 copy-start.2
  7.2 0.0 all-gather.6.cloned.1.call-start
  7.2 0.7 all-gather.6.cloned.1.call-update
  7.9 0.0 all-gather.4.cloned.1.call-start
  8.0 0.7 all-gather.4.cloned.1.call-update
  8.7 0.0 all-reduce.2.cloned.1.call-start
  8.7 3.4 %fusion.7 = f32[768,64]{0,1:T(8,128)S(1)} fusion(bf16[768,2560]{1,0:T(8,128)(2,1)} %param.7, bf16[64,2560]{1,0:T(8,128)(2,1)} %param.10), kind=kOutput, calls=%fused_computation.10 | convolution fusion | flops 251658240 | bytes 4456448 | tf_op jit(solution)/shard_map/tf,kf->tk/dot_general | solution.py:13
  12.2 0.7 copy.22
  12.9 0.0 all-reduce.2.cloned.1.call-update
  12.9 21.6 %all-gather.6.cloned.1.call-done = bf16[64,8192]{1,0:T(8,128)(2,1)} async-done(((bf16[64,1024]{1,0:T(8,128)(2,1)}), bf16[64,8192]{1,0:T(8,128)(2,1)}) %all-gather.6.cloned.1.call-update) | async-done | bytes 1048592 | tf_op jit(solution)/shard_map/all_gather | solution.py:15
  34.5 118.0 %all-gather.4.cloned.1.call-done = bf16[768,8192]{1,0:T(8,128)(2,1)} async-done(((bf16[768,1024]{1,0:T(8,128)(2,1)}), bf16[768,8192]{1,0:T(8,128)(2,1)}) %all-gather.4.cloned.1.call-update) | async-done | bytes 12582928 | tf_op jit(solution)/shard_map/all_gather | solution.py:14
  152.5 8.7 %fusion.8 = f32[768,64]{0,1:T(8,128)S(1)} fusion(bf16[768,8192]{1,0:T(8,128)(2,1)} %all-gather.4.cloned.1.call-done, bf16[64,8192]{1,0:T(8,128)(2,1)} %all-gather.6.cloned.1.call-done), kind=kOutput, calls=%fused_computation.11 | convolution fusion | flops 805306368 | bytes 13828096 | tf_op jit(solution)/shard_map/td,kd->tk/dot_general | solution.py:17
  161.2 47.0 %all-reduce.2.cloned.1.call-done = f32[3,256,64]{1,2,0:T(8,128)} async-done(((f32[3,256,64]{1,2,0:T(8,128)}), f32[3,256,64]{1,2,0:T(8,128)}) %all-reduce.2.cloned.1.call-update) | async-done | bytes 196624 | tf_op jit(solution)/shard_map/psum | solution.py:18
  208.2 1.2 fusion
  209.4 0.1 reshape.21
  209.5 9.3 %all-gather = f32[4,3,4096]{2,1,0:T(4,128)S(1)} all-gather(f32[1,3,4096]{2,1,0:T(4,128)S(1)} %reshape.21), channel_id=1, replica_groups=mesh['dp'=4,'tensor'=8] {'dp'}, dimensions={0}, use_global_device_ids=true | all-gather | bytes 245760 | tf_op jit(solution)/shard_map/all_gather | solution.py:27
  218.9 0.1 reshape.22
  219.0 0.0 copy-done.2
  219.0 0.3 fusion.3
  219.2 0.0 copy-done
  219.2 1.5 fusion.9
  220.7 41.4 %convolution_convert_fusion = bf16[768,2560]{1,0:T(8,128)(2,1)} fusion(bf16[768,8192]{1,0:T(8,128)(2,1)} %all-gather.4.cloned.1.call-done, bf16[2560,8192]{1,0:T(8,128)(2,1)} %param.9), kind=kOutput, calls=%fused_computation | convolution fusion | flops 32214220800 | bytes 58458112 | tf_op jit(solution)/shard_map/td,fd->tf/dot_general | solution.py:16
  262.1 0.0 copy-done.1
  (2 shorter events, 0.0 us)
Async XLA Ops:
  7.2 212.1 %copy-start = (bf16[128,4096]{1,0:T(8,128)(2,1)S(1)}, bf16[128,4096]{1,0:T(8,128)(2,1)}, u32[]{:S(2)}) copy-start(bf16[128,4096]{1,0:T(8,128)(2,1)} %param.12) | copy-start | bytes 3145732
  7.2 211.8 %copy-start.2 = (s32[12]{0:T(128)S(1)}, s32[12]{0:T(128)}, u32[]{:S(2)}) copy-start(s32[12]{0:T(128)} %param.13) | copy-start | bytes 148
  7.2 27.3 %all-gather.6.cloned.1.call-start = ((), (), s32[]{:S(2)}) async-start(), calls=%async_computation.2 | async-start | bytes 1179648 | tf_op jit(solution)/shard_map/all_gather | solution.py:15
  7.9 144.5 %all-gather.4.cloned.1.call-start = ((), (), s32[]{:S(2)}) async-start(), calls=%async_computation | async-start | bytes 14155776 | tf_op jit(solution)/shard_map/all_gather | solution.py:14
  8.7 199.5 %all-reduce.2.cloned.1.call-start = ((), (), s32[]{:S(2)}) async-start(), calls=%async_computation.1 | async-start | bytes 393216 | tf_op jit(solution)/shard_map/psum | solution.py:18
  220.7 41.4 %copy-start.1 = (bf16[128,4096]{1,0:T(8,128)(2,1)S(1)}, bf16[128,4096]{1,0:T(8,128)(2,1)}, u32[]{:S(2)}) copy-start(bf16[128,4096]{1,0:T(8,128)(2,1)} %param.12) | copy-start | bytes 3145732
Sparse Core Ops, SparseCore 0:
  9.6 24.7 all-gather.5
  36.1 116.3 all-gather.3
  155.4 52.7 all-reduce.1
where the time goes:
time: 269 us
  waiting for transfers between devices  188 us (70%)
  matrix products  56.5 us (21%)
  between operations  13.8 us (5%)
  blocking collectives  9.3 us (3%)
    all_gather x1, waiting for transfers between devices, on_device(): grad_piece = lax.all_gather(out_grad, 'tensor', axis=1, tiled=True)  118 us
    psum x1, waiting for transfers between devices, on_device(): act_low = lax.psum(act_part, 'tensor')  47 us
    dot_general x1, matrix products, on_device(): jnp.einsum('td,fd->tf', grad_piece, w_down, preferred_element_type=jnp.fl...  41.4 us
    all_gather x1, waiting for transfers between devices, on_device(): proj_piece = lax.all_gather(proj_out, 'tensor', axis=1, tiled=True)  21.6 us
    all_gather x1, blocking collectives, on_device(): all_grads = lax.all_gather(proj_grads, 'dp', axis=0, tiled=True)  9.3 us
    dot_general x1, matrix products, on_device(): jnp.einsum('td,kd->tk', grad_piece, proj_piece, preferred_element_type=jn...  8.72 us
  transfers between devices with their start and end apart: 3, of which 3 were waited for; matrix products, arithmetic and copies ran while one was open for 5% of the time, Pallas kernels for 0%

commit v1 on v0

--- a/solution.py
+++ b/solution.py
@@ -11,12 +11,15 @@
     tok_rows = hidden.shape[0]
     seq_count = tok_rows // LEN
     act_part = jnp.einsum("tf,kf->tk", hidden, proj_in, preferred_element_type=jnp.float32)
-    grad_piece = lax.all_gather(out_grad, "tensor", axis=1, tiled=True)
-    proj_piece = lax.all_gather(proj_out, "tensor", axis=1, tiled=True)
-    first = jnp.einsum("td,fd->tf", grad_piece, w_down, preferred_element_type=jnp.float32)
-    second = jnp.einsum("td,kd->tk", grad_piece, proj_piece, preferred_element_type=jnp.float32)
-    act_low = lax.psum(act_part, "tensor")
-    input_grad = first.astype(jnp.bfloat16)
+    grad_part = jnp.einsum("td,kd->tk", out_grad, proj_out, preferred_element_type=jnp.float32)
+    low = lax.psum(jnp.concatenate([act_part, grad_part], axis=1), "tensor")
+    act_low, second = jnp.split(low, 2, axis=1)
+    blocks = []
+    for start in range(0, tok_rows, LEN):
+        piece = lax.all_gather(out_grad[start:start + LEN], "tensor", axis=1, tiled=True)
+        first = jnp.einsum("td,fd->tf", piece, w_down, preferred_element_type=jnp.float32)
+        blocks.append(first.astype(jnp.bfloat16))
+    input_grad = jnp.concatenate(blocks, axis=0)
     width = act_low.shape[1]
     act_seq = act_low.reshape(seq_count, LEN, width)
     grad_seq = second.reshape(seq_count, LEN, width)

time: 269 us -> 241 us (0.90)
  waiting for transfers between devices: 188 us -> 149 us
  matrix products: 56.5 us -> 62.8 us
  other arithmetic: 0.01 us -> 2.85 us
    all_gather x2 -> x3, waiting for transfers between devices: 140 us -> 92.5 us  [on_device(): lax.all_gather(out_grad[start:start + LEN], 'tensor', axis=1, tiled=True)]
    psum x1, waiting for transfers between devices: 47 us -> 55.7 us  [on_device(): low = lax.psum(jnp.concatenate([act_part, grad_part], axis=1), 'tensor')]
    dot_general x2 -> x4, matrix products: 50.1 us -> 57.1 us  [the longest x3 56.5 us: on_device(): jnp.einsum('td,fd->tf', piece, w_down, preferred_element_type=jnp.float32)]
    concatenate x0 -> x2, other arithmetic: none -> 2.84 us  [the longest x1 2.07 us: on_device(): input_grad = jnp.concatenate(blocks, axis=0)]
  transfers between devices with their start and end apart: 3 -> 4, of which waited for: 3 -> 4; matrix products, arithmetic and copies ran while one was open for 5% -> 18% of each run, Pallas kernels for 0% -> 0%
where the time goes in v1:
time: 241 us
  waiting for transfers between devices  149 us (62%)
  matrix products  62.8 us (26%)
  between operations  13.9 us (6%)
  blocking collectives  9.21 us (4%)
  other arithmetic  2.85 us (1%)
  local copies, waits for them, and re-layouts  2.46 us (1%)
    all_gather x3, waiting for transfers between devices, on_device(): lax.all_gather(out_grad[start:start + LEN], 'tensor', axis=1, tiled=True)  92.5 us
    dot_general x3, matrix products, on_device(): jnp.einsum('td,fd->tf', piece, w_down, preferred_element_type=jnp.float32)  56.5 us
    psum x1, waiting for transfers between devices, on_device(): low = lax.psum(jnp.concatenate([act_part, grad_part], axis=1), 'tensor')  55.7 us
    all_gather x1, blocking collectives, on_device(): all_grads = lax.all_gather(proj_grads, 'dp', axis=0, tiled=True)  9.21 us
  transfers between devices with their start and end apart: 4, of which 4 were waited for; matrix products, arithmetic and copies ran while one was open for 18% of the time, Pallas kernels for 0%

profile of v1, /device:TPU:0, one launch (start us, length us, event | category | flops | bytes accessed | tf_op | source)
XLA Modules:
  0.0 240.9 jit_solution(5313632173947948702)
XLA Ops:
  7.2 0.0 all-reduce.2.cloned.1.call-start
  7.2 3.6 %fusion.11 = f32[768,64]{0,1:T(8,128)S(1)} fusion(bf16[768,2560]{1,0:T(8,128)(2,1)} %param.7, bf16[64,2560]{1,0:T(8,128)(2,1)} %param.10), kind=kOutput, calls=%fused_computation.17 | convolution fusion | flops 251658240 | bytes 4456448 | tf_op jit(solution)/shard_map/tf,kf->tk/dot_general | solution.py:13
  10.9 0.6 fusion.12
  11.5 0.8 pad_maximum_fusion.1
  12.3 0.0 all-gather.9.cloned.1.call-start
  12.3 1.2 fusion.9
  13.5 0.0 all-gather.7.cloned.1.call-start
  13.6 0.7 all-gather.7.cloned.1.call-update
  14.3 0.5 all-gather.5.cloned.1.call-update
  14.9 55.7 %all-reduce.2.cloned.1.call-done = f32[768,128]{0,1:T(8,128)} async-done(((f32[768,128]{0,1:T(8,128)}), f32[768,128]{0,1:T(8,128)}) %all-reduce.2.cloned.1.call-update) | async-done | bytes 393232 | tf_op jit(solution)/shard_map/psum | solution.py:15
  70.6 1.0 fusion.10
  71.6 0.3 fusion
  72.0 0.1 reshape.21
  72.1 9.2 %all-gather = f32[4,3,4096]{2,1,0:T(4,128)S(1)} all-gather(f32[1,3,4096]{2,1,0:T(4,128)S(1)} %reshape.21), channel_id=1, replica_groups=mesh['dp'=4,'tensor'=8] {'dp'}, dimensions={0}, use_global_device_ids=true | all-gather | bytes 245760 | tf_op jit(solution)/shard_map/all_gather | solution.py:30
  81.3 0.1 reshape.22
  81.4 0.3 fusion.5
  81.7 1.5 fusion.13
  83.2 35.3 %all-gather.9.cloned.1.call-done = bf16[256,8192]{1,0:T(8,128)(2,1)} async-done(((bf16[256,1024]{1,0:T(8,128)(2,1)}), bf16[256,8192]{1,0:T(8,128)(2,1)}) %all-gather.9.cloned.1.call-update) | async-done | bytes 4194320 | tf_op jit(solution)/shard_map/all_gather | solution.py:19
  118.4 18.7 %convolution_convert_fusion = bf16[256,2560]{1,0:T(8,128)(2,1)S(1)} fusion(bf16[256,8192]{1,0:T(8,128)(2,1)} %all-gather.9.cloned.1.call-done, bf16[2560,8192]{1,0:T(8,128)(2,1)} %param.9), kind=kOutput, calls=%fused_computation.1 | convolution fusion | flops 10738073600 | bytes 47448064 | tf_op jit(solution)/shard_map/td,fd->tf/dot_general | solution.py:20
  137.1 29.4 %all-gather.7.cloned.1.call-done = bf16[256,8192]{1,0:T(8,128)(2,1)} async-done(((bf16[256,1024]{1,0:T(8,128)(2,1)}), bf16[256,8192]{1,0:T(8,128)(2,1)}) %all-gather.7.cloned.1.call-update) | async-done | bytes 4194320 | tf_op jit(solution)/shard_map/all_gather | solution.py:19
  166.6 19.6 %convolution_convert_fusion.1 = bf16[256,2560]{1,0:T(8,128)(2,1)} fusion(bf16[256,8192]{1,0:T(8,128)(2,1)} %all-gather.7.cloned.1.call-done, bf16[2560,8192]{1,0:T(8,128)(2,1)} %param.9), kind=kOutput, calls=%fused_computation.2 | convolution fusion | flops 10738073600 | bytes 47448064 | tf_op jit(solution)/shard_map/td,fd->tf/dot_general | solution.py:20
  186.2 27.8 %all-gather.5.cloned.1.call-done = bf16[256,8192]{1,0:T(8,128)(2,1)} async-done(((bf16[256,1024]{1,0:T(8,128)(2,1)}), bf16[256,8192]{1,0:T(8,128)(2,1)}) %all-gather.5.cloned.1.call-update) | async-done | bytes 4194320 | tf_op jit(solution)/shard_map/all_gather | solution.py:19
  214.0 18.2 %convolution_convert_fusion.2 = bf16[256,2560]{1,0:T(8,128)(2,1)S(1)} fusion(bf16[256,8192]{1,0:T(8,128)(2,1)} %all-gather.5.cloned.1.call-done, bf16[2560,8192]{1,0:T(8,128)(2,1)} %param.9), kind=kOutput, calls=%fused_computation.3 | convolution fusion | flops 10738073600 | bytes 47448064 | tf_op jit(solution)/shard_map/td,fd->tf/dot_general | solution.py:20
  232.3 2.1 pad_maximum_fusion
  (16 shorter events, 0.1 us)
Async XLA Ops:
  7.2 74.5 %copy-start = (bf16[128,4096]{1,0:T(8,128)(2,1)S(1)}, bf16[128,4096]{1,0:T(8,128)(2,1)}, u32[]{:S(2)}) copy-start(bf16[128,4096]{1,0:T(8,128)(2,1)} %param.12) | copy-start | bytes 3145732
  7.2 3.7 %copy-start.2 = (bf16[768,1024]{1,0:T(8,128)(2,1)S(1)}, bf16[768,1024]{1,0:T(8,128)(2,1)}, u32[]{:S(2)}) copy-start(bf16[768,1024]{1,0:T(8,128)(2,1)} %param.8) | copy-start | bytes 4718596
  7.2 3.7 %copy-start.4 = (bf16[64,1024]{1,0:T(8,128)(2,1)S(1)}, bf16[64,1024]{1,0:T(8,128)(2,1)}, u32[]{:S(2)}) copy-start(bf16[64,1024]{1,0:T(8,128)(2,1)} %param.11) | copy-start | bytes 393220
  7.2 63.4 %all-reduce.2.cloned.1.call-start = ((), (), s32[]{:S(2)}) async-start(), calls=%async_computation.3 | async-start | bytes 786432 | tf_op jit(solution)/shard_map/psum | solution.py:15
  11.5 69.9 %copy-start.5 = (s32[12]{0:T(128)S(1)}, s32[12]{0:T(128)}, u32[]{:S(2)}) copy-start(s32[12]{0:T(128)} %param.13) | copy-start | bytes 148
  12.3 106.2 %all-gather.9.cloned.1.call-start = ((), (), s32[]{:S(2)}) async-start(), calls=%async_computation.2 | async-start | bytes 4718592 | tf_op jit(solution)/shard_map/all_gather | solution.py:19
  13.5 153.1 %all-gather.7.cloned.1.call-start = ((), (), s32[]{:S(2)}) async-start(), calls=%async_computation.1 | async-start | bytes 4718592 | tf_op jit(solution)/shard_map/all_gather | solution.py:19
  14.3 199.7 %all-gather.5.cloned.1.call-start = ((), (), s32[]{:S(2)}) async-start(), calls=%async_computation | async-start | bytes 4718592 | tf_op jit(solution)/shard_map/all_gather | solution.py:19
  214.0 18.2 %copy-start.3 = (bf16[256,2560]{1,0:T(8,128)(2,1)S(1)}, bf16[256,2560]{1,0:T(8,128)(2,1)}, u32[]{:S(2)}) copy-start(bf16[256,2560]{1,0:T(8,128)(2,1)} %convolution_convert_fusion.1) | copy-start | bytes 3932164
  214.0 20.3 %copy-start.1 = (bf16[128,4096]{1,0:T(8,128)(2,1)S(1)}, bf16[128,4096]{1,0:T(8,128)(2,1)}, u32[]{:S(2)}) copy-start(bf16[128,4096]{1,0:T(8,128)(2,1)} %param.12) | copy-start | bytes 3145732
Sparse Core Ops, SparseCore 0:
  12.4 58.1 all-reduce.1
  72.3 46.1 all-gather.8
  120.7 45.8 all-gather.6
  168.1 45.8 all-gather.4
